TPU v7x, 512 devices: a whole 4x8x8 slice. The times are simulated.
512 devices in a mesh: blk: 16 (over y, z_lo), band: 32 (over x, z_hi, core).
Axes of the slice: x: 4, y: 8, z: 8 (z_hi: 4, z_lo: 2; z = z_hi * 2 + z_lo), core: 2. Of those that a mesh axis runs over, the one named last changes fastest.
Arguments:
- waveforms: bfloat16 [32, 1024, 3000], P('band', 'blk'), may hold values from -200 to 200
Outputs:
- cross: bfloat16 [2, 384, 1024, 1024], P(None, 'band', 'blk')
All inputs are finite; a program needn't handle non-finite values.
Results may differ from a plain program's by a relative error of at most 0.0072.
Values may be sent and summed in bfloat16 or wider, within the bound.
A program may use at most 64 MiB of HBM per device.

v0:
```python
import math

import jax
import jax.numpy as jnp
from jax import lax
from jax.sharding import PartitionSpec as P

BINS = 384
HALF = 64


def make_table(length):
    samples = jnp.arange(length, dtype=jnp.int32)
    freqs = jnp.arange(1, BINS + 1, dtype=jnp.int32)
    phase = (freqs[:, None] * samples[None, :] % length).astype(jnp.float32) * (
        2.0 * math.pi / length
    )
    return jnp.concatenate([jnp.cos(phase), -jnp.sin(phase)], axis=0).astype(jnp.bfloat16)


def make_band():
    freqs = jnp.arange(BINS, dtype=jnp.int32)
    near = (jnp.abs(freqs[:, None] - freqs[None, :]) <= HALF).astype(jnp.float32)
    return near / jnp.sum(near, axis=1, keepdims=True)


def pair_tile(own_both, piece, scale):
    width = own_both.shape[2] // 2
    other = piece.shape[3]
    piece_both = jnp.concatenate([piece[0], piece[1]], axis=2)
    products = jnp.einsum("fsa,fsb->fab", own_both, piece_both, preferred_element_type=jnp.float32)
    real_sum = products[:, :width, :other] + products[:, width:, other:]
    imag_sum = products[:, width:, :other] - products[:, :width, other:]
    return jnp.stack([real_sum, imag_sum]) * scale


def shards(waveforms):
    seg_dev, block, length = waveforms.shape
    values = waveforms.astype(jnp.float32)
    centred = values - jnp.mean(values, axis=2, keepdims=True)
    normed = (
        centred * lax.rsqrt(jnp.mean(centred * centred, axis=2, keepdims=True) + 1e-05)
    ).astype(jnp.bfloat16)
    table = make_table(length)
    raw = lax.dot_general(
        table, normed, (((1,), (2,)), ((), ())), preferred_element_type=jnp.float32
    )
    raw = raw.reshape(2, BINS, seg_dev, block)
    power = raw[0] * raw[0] + raw[1] * raw[1]
    smooth = jnp.einsum("fg,gsi->fsi", make_band(), power, precision=lax.Precision.HIGHEST)
    spectra = (raw * lax.rsqrt(smooth + 1e-05)[None]).astype(jnp.bfloat16)
    local = lax.all_to_all(spectra, "band", split_axis=1, concat_axis=2, tiled=True)
    segments = local.shape[2]
    scale = 1.0 / segments
    own_both = jnp.concatenate([local[0], local[1]], axis=2)
    tile = pair_tile(own_both, lax.all_gather(local, "blk", axis=3, tiled=True), scale)
    return tile.astype(jnp.bfloat16)


def solution(mesh):
    return jax.shard_map(
        shards,
        mesh=mesh,
        in_specs=(P("band", "blk", None),),
        out_specs=P(None, "band", "blk", None),
        check_vma=False,
    )
```

profile of v0, /device:TPU:6, one launch (start us, length us, event | category | flops | bytes accessed | tf_op | source)
XLA Modules:
  0.0 249.4 jit_solution(15828708618752721093)
XLA Ops:
  6.5 0.0 copy-start
  6.5 0.0 all-gather.3.cloned.1.call-start
  6.5 0.2 convert_reduce_fusion.1
  6.7 1.2 convert_reduce_fusion
  7.9 1.3 fusion.19
  9.2 20.3 %cosine_convert_fusion = (bf16[384,3000]{1,0:T(8,128)(2,1)S(1)}, bf16[384,3000]{1,0:T(8,128)(2,1)S(1)}) fusion(s32[384]{0:T(512)S(1)} %iota_add_fusion), kind=kLoop, calls=%fused_computation.10 | loop fusion | flops 13824000 | bytes 4609536 | tf_op jit(solution)/shard_map/convert
  29.4 0.0 copy-done
  29.4 1.6 fusion.3
  31.0 0.1 reshape.72
  31.1 0.9 fusion.16
  32.0 0.2 copy.23
  32.2 0.1 reshape.78
  32.4 21.6 %all_to_all.18 = bf16[32,2,768]{2,1,0:T(2,128)(2,1)S(1)} all-to-all(bf16[32,2,768]{2,1,0:T(2,128)(2,1)S(1)} %reshape.78), channel_id=1, replica_groups=mesh['blk'=16,'band'=32] {'band'}, dimensions={0} | all-to-all | bytes 196608 | tf_op jit(solution)/shard_map/all_to_all | solution.py:52
  54.0 0.2 reshape.79
  54.2 1.0 copy.25
  55.2 0.0 all-gather.3.cloned.1.call-update
  55.2 140.8 %all-gather.3.cloned.1.call-done = bf16[2,12,32,1,1024]{2,0,3,1,4:T(2,128)(2,1)} async-done(((bf16[2,12,32,1,64]{2,0,3,1,4:T(2,128)(2,1)}), bf16[2,12,32,1,1024]{2,0,3,1,4:T(2,128)(2,1)}) %all-gather.3.cloned.1.call-update) | async-done | bytes 1572880 | tf_op jit(solution)/shard_map/all_gather | solution.py:56
  196.0 13.9 %fusion.36 = (bf16[1,12,32,1,1024]{2,0,3,1,4:T(2,128)(2,1)}, bf16[1,12,32,1,1024]{2,0,3,1,4:T(2,128)(2,1)}) fusion(bf16[2,12,32,1,1024]{2,0,3,1,4:T(2,128)(2,1)} %all-gather.3.cloned.1.call-done), kind=kLoop, calls=%fused_computation.56 | loop fusion | bytes 3145728 | tf_op jit(solution)/shard_map/slice | solution.py:30
  209.9 12.9 %copy.28 = bf16[1,12,32,1,1024]{4,2,1,3,0:T(8,128)(2,1)S(1)} copy(bf16[1,12,32,1,1024]{2,0,3,1,4:T(2,128)(2,1)} %get-tuple-element.7) | data formatting | bytes 1572864
  222.8 12.9 %copy.29 = bf16[1,12,32,1,1024]{4,2,1,3,0:T(8,128)(2,1)S(1)} copy(bf16[1,12,32,1,1024]{2,0,3,1,4:T(2,128)(2,1)} %get-tuple-element.8) | data formatting | bytes 1572864
  235.8 1.9 fusion.12
  237.7 2.2 fusion.11
  239.9 2.6 %fusion = bf16[2,12,64,1024]{3,2,1,0:T(8,128)(2,1)} fusion(f32[1,12,64,1024]{3,2,1,0:T(8,128)S(1)} %get-tuple-element.6, f32[1,12,64,1024]{3,2,1,0:T(8,128)S(1)} %get-tuple-element.5), kind=kLoop, calls=%fused_computation.2 | loop fusion | flops 4718592 | bytes 9437184 | tf_op jit(solution)/shard_map/convert_element_type | solution.py:57
  (6 shorter events, 0.1 us)
Async XLA Ops:
  6.5 22.9 %copy-start = (bf16[1,64,3000]{2,1,0:T(8,128)(2,1)S(1)}, bf16[1,64,3000]{2,1,0:T(8,128)(2,1)}, u32[]{:S(2)}) copy-start(bf16[1,64,3000]{2,1,0:T(8,128)(2,1)} %param.1) | copy-start | bytes 1152004
  6.5 189.5 %all-gather.3.cloned.1.call-start = ((), (), s32[]{:S(2)}) async-start(), calls=%async_computation.1 | async-start | bytes 6684672 | tf_op jit(solution)/shard_map/all_gather | solution.py:56
Sparse Core Ops, SparseCore 0:
  55.3 140.6 all-gather.2
where the time goes:
time: 252 us; the launch traced here: 249 us
  waiting for transfers between devices  141 us (56%)
  local copies, waits for them, and re-layouts  41.4 us (16%)
  other arithmetic  27.7 us (11%)
  blocking collectives  21.6 us (9%)
  between operations  13.5 us (5%)
  matrix products  4.33 us (2%)
    all_gather x1, waiting for transfers between devices, shards(): lax.all_gather(local, 'blk', axis=3, tiled=True)  141 us
    unnamed x6, local copies, waits for them, and re-layouts  26.2 us
    all_to_all x1, blocking collectives, shards(): lax.all_to_all(spectra, 'band', split_axis=1, concat_axis=2, tiled=True)  21.6 us
    another operation x1, other arithmetic  20.3 us
    slice x1, local copies, waits for them, and re-layouts, pair_tile(): piece_both = jnp.concatenate([piece[0], piece[1]], axis=2)  13.9 us
  transfers between devices with their start and end apart: 1, of which 1 were waited for; matrix products, arithmetic and copies ran while one was open for 0% of the time, Pallas kernels for 0%

commit v1 on v0

v1 whole, which is shorter than its diff:
```python
import functools
import math

import jax
import jax.numpy as jnp
import numpy as np
import ml_dtypes
from jax import lax
from jax.experimental import pallas as pl
from jax.experimental.pallas import tpu as pltpu
from jax.sharding import PartitionSpec as P

L = 3000
BINS = 384
HALF = 64
QUARTER = 750
QPAD = 768
SPAD = 3072
PER = 12
ROWS = 16
NSEG = 32
NY = 8
MESH = pl.DeviceIdType.MESH
DCH, ECH = 0, 1
HALFBINS = PER // 2


def make_table():
    freqs = np.arange(1, BINS + 1, dtype=np.int64)
    samples = np.arange(QUARTER, dtype=np.int64)
    phase = ((freqs[:, None] * samples[None, :]) % L).astype(np.float64) * (2.0 * math.pi / L)
    table = np.zeros((2 * BINS, QPAD), np.float32)
    table[:BINS, :QUARTER] = np.cos(phase)
    table[BINS:, :QUARTER] = -np.sin(phase)
    return table.astype(ml_dtypes.bfloat16)


def ring_goes(step, direction, kind):
    if step <= 3:
        return True
    if step > 4:
        return False
    return (kind == 1) if direction else (kind != 1)


KINDS = ((0, ECH), (0, DCH), (1, DCH))


def whiten(xv, tv, n32, x4, zs, spec, send, table_ready):
    for block in range(4):
        rows = pl.ds(16 * block, 16)
        values = xv[rows, :].astype(jnp.float32)
        centred = values - jnp.sum(values, axis=1, keepdims=True) * (1.0 / L)
        var = jnp.sum(centred * centred, axis=1, keepdims=True) * (1.0 / L)
        n32[rows, SPAD - 128 :] = jnp.zeros((16, 128), jnp.float32)
        n32[rows, :L] = centred * lax.rsqrt(var + 1e-05)
        x4[rows, :] = n32[rows, :QPAD].astype(jnp.bfloat16)
        for q in range(1, 4):
            start = QUARTER * q // 128 * 128
            off = QUARTER * q - start
            window = n32[rows, start : start + 896]
            window = pltpu.roll(window, 896 - off, 1)
            x4[pl.ds(64 * q + 16 * block, 16), :] = window[:, :QPAD].astype(jnp.bfloat16)

    table_ready()
    zs[...] = lax.dot_general(
        tv[...], x4[...], (((1,), (1,)), ((), ())), preferred_element_type=jnp.float32
    )

    shape = (96, 128)
    row = lax.broadcasted_iota(jnp.int32, shape, 0)
    lane = lax.broadcasted_iota(jnp.int32, shape, 1)
    low = lane < 64
    phase = row % 4
    even = phase % 2 == 1
    sigma = jnp.where(even, 1.0, -1.0)
    kappa = jnp.where(
        phase == 1, -1.0, jnp.where(phase == 3, 1.0, jnp.where((phase == 0) == low, 1.0, -1.0))
    )
    for part in range(4):
        rows = slice(96 * part, 96 * part + 96)
        irows = slice(BINS + 96 * part, BINS + 96 * part + 96)
        a_sum = zs[rows, :128] + sigma * zs[rows, 128:]
        b_sum = zs[irows, :128] + sigma * zs[irows, 128:]
        a_roll = pltpu.roll(a_sum, 64, 1)
        b_roll = pltpu.roll(b_sum, 64, 1)
        first = jnp.where(low, a_sum, b_roll)
        other = jnp.where(
            even, jnp.where(low, a_roll, b_sum), jnp.where(low, b_roll, a_sum)
        )
        raw = first + kappa * other
        spec[rows, :] = raw
        square = raw * raw
        power = square + pltpu.roll(square, 64, 1)
        high = power.astype(jnp.bfloat16).astype(jnp.float32)
        n32[rows, :128] = jnp.where(low, high, power - high)

    frow = lax.broadcasted_iota(jnp.int32, (BINS, BINS), 0)
    gcol = lax.broadcasted_iota(jnp.int32, (BINS, BINS), 1)
    near = jnp.where(jnp.abs(frow - gcol) <= HALF, 1.0, 0.0).astype(jnp.bfloat16)
    total = jnp.dot(
        near, n32[:BINS, :128].astype(jnp.bfloat16), preferred_element_type=jnp.float32
    )
    frow = lax.broadcasted_iota(jnp.int32, (BINS, 128), 0)
    count = jnp.minimum(frow + HALF, BINS - 1) - jnp.maximum(frow - HALF, 0) + 1
    smooth = (total + pltpu.roll(total, 64, 1)) / count.astype(jnp.float32)
    spec[:BINS, :] = spec[:BINS, :] * lax.rsqrt(smooth + 1e-05)
    spec[BINS:, :] = jnp.zeros((8, 128), jnp.float32)
    for dev in range(NSEG):
        send[dev] = spec[pl.ds(PER * dev, ROWS), :].astype(jnp.bfloat16)


def kernel(
    x_hbm, t_hbm, o_ref,
    xv, tv, n32, x4, zs, spec, send, recv, r32, gath, wt,
    in_sem, a_send, a_recv, y_send, y_recv, z_send, z_recv,
):
    blk = lax.axis_index("blk")
    band = lax.axis_index("band")
    yy = blk // 2
    zz = lax.rem(blk, 2)
    right = lax.rem(yy + 1, NY) * 2 + zz
    left = lax.rem(yy + NY - 1, NY) * 2 + zz
    partner = yy * 2 + 1 - zz

    x_copy = pltpu.make_async_copy(x_hbm.at[0], xv, in_sem.at[0])
    t_copy = pltpu.make_async_copy(t_hbm, tv, in_sem.at[1])
    x_copy.start()
    t_copy.start()

    barrier = pltpu.get_barrier_semaphore()
    for other in (left, right, partner):
        pl.semaphore_signal(barrier, inc=1, device_id={"blk": other, "band": band}, device_id_type=MESH)

    def greet(k, carry):
        pl.semaphore_signal(
            barrier,
            inc=1,
            device_id={"blk": blk, "band": lax.rem(band + k, NSEG)},
            device_id_type=MESH,
        )
        return carry

    lax.fori_loop(1, NSEG, greet, 0)

    x_copy.wait()
    whiten(xv, tv, n32, x4, zs, spec, send, t_copy.wait)

    pl.semaphore_wait(barrier, 3 + NSEG - 1)

    def scatter(k, carry):
        to = lax.rem(band + k, NSEG)
        pltpu.make_async_remote_copy(
            src_ref=send.at[to],
            dst_ref=recv.at[k],
            send_sem=a_send,
            recv_sem=a_recv,
            device_id={"blk": blk, "band": to},
            device_id_type=MESH,
        ).start()
        return carry

    lax.fori_loop(1, NSEG, scatter, 0)
    recv[0] = send[band]
    rest = pl.ds(1, NSEG - 1)
    pltpu.make_async_copy(recv.at[rest], recv.at[rest], a_recv).wait()

    for seg in range(NSEG):
        r32[pl.ds(ROWS * seg, ROWS), :] = recv[seg].astype(jnp.float32)
    for f in range(PER):
        gath[0, 0, f] = r32[pl.ds(f, NSEG, stride=ROWS), :].astype(jnp.bfloat16)

    def bins(half):
        return pl.ds(HALFBINS * half, HALFBINS)

    started = []

    def z_copy(slot, half):
        return pltpu.make_async_remote_copy(
            src_ref=gath.at[0, slot, bins(half)],
            dst_ref=gath.at[1, slot, bins(half)],
            send_sem=z_send.at[slot, half],
            recv_sem=z_recv.at[slot, half],
            device_id={"blk": partner, "band": band},
            device_id_type=MESH,
        )

    def y_copy(step, direction, kind):
        plane, half = KINDS[kind]
        source = (step - 1) if direction == 0 else (NY - step + 1) % NY
        target = step if direction == 0 else NY - step
        return pltpu.make_async_remote_copy(
            src_ref=gath.at[plane, source, bins(half)],
            dst_ref=gath.at[plane, target, bins(half)],
            send_sem=y_send.at[step - 1, direction, kind],
            recv_sem=y_recv.at[step - 1, direction, kind],
            device_id={"blk": (right, left)[direction], "band": band},
            device_id_type=MESH,
        )

    def start(copy):
        copy.start()
        started.append(copy)

    def stack(slots, half):
        lanes = [
            pl.ds(pl.multiple_of(lax.rem(yy + NY - slot, NY) * 128, 128), 128) for slot in slots
        ]

        def one(f, carry):
            for slot, columns in zip(slots, lanes):
                g0 = gath[zz, slot, f]
                g1 = gath[1 - zz, slot, f]
                top = jnp.concatenate([g0[:, :64], g1[:, :64]], axis=1)
                bottom = jnp.concatenate([g0[:, 64:], g1[:, 64:]], axis=1)
                both = jnp.concatenate([top, bottom], axis=0)
                out = jnp.dot(wt[f], both, preferred_element_type=jnp.float32)
                out = out.astype(jnp.bfloat16)
                o_ref[0, f, :, columns] = out[:64]
                o_ref[1, f, :, columns] = out[64:]
            return carry

        lax.fori_loop(HALFBINS * half, HALFBINS * half + HALFBINS, one, 0)

    start(z_copy(0, DCH))
    for kind in (0, 1):
        for direction in (0, 1):
            start(y_copy(1, direction, kind))
    start(z_copy(0, ECH))

    wlow = lax.broadcasted_iota(jnp.int32, (NSEG, 128), 1) < 64
    for f in range(PER):
        own = r32[pl.ds(f, NSEG, stride=ROWS), :] * (1.0 / NSEG)
        turned = pltpu.roll(own, 64, 1)
        turned = jnp.where(wlow, turned, -turned)
        wt[f] = jnp.transpose(jnp.concatenate([own, turned], axis=0)).astype(jnp.bfloat16)

    z_copy(0, DCH).wait_recv()
    for direction in (0, 1):
        start(y_copy(1, direction, 2))
    stack((0,), DCH)

    previous = (0,)
    for step in range(1, 5):
        for kind, (plane, half) in enumerate(KINDS):
            for direction in (0, 1):
                if not ring_goes(step, direction, kind):
                    continue
                slot = step if direction == 0 else NY - step
                y_copy(step, direction, kind).wait_recv()
                if ring_goes(step + 1, direction, kind):
                    start(y_copy(step + 1, direction, kind))
                if plane == 0 and half == ECH:
                    start(z_copy(slot, ECH))
        for slot in previous:
            z_copy(slot, ECH).wait_recv()
        stack(previous, ECH)
        slots = (step, NY - step) if step < 4 else (4,)
        stack(slots, DCH)
        previous = slots
    for slot in previous:
        z_copy(slot, ECH).wait_recv()
    stack(previous, ECH)

    for copy in started:
        copy.wait_send()
    pltpu.make_async_copy(send.at[rest], send.at[rest], a_send).wait()


def shards(waveforms):
    table = jnp.asarray(make_table())
    bf16, f32 = jnp.bfloat16, jnp.float32
    return pl.pallas_call(
        kernel,
        out_shape=jax.ShapeDtypeStruct((2, PER, 64, 1024), bf16),
        in_specs=[pl.BlockSpec(memory_space=pl.ANY)] * 2,
        out_specs=pl.BlockSpec(memory_space=pltpu.VMEM),
        scratch_shapes=[
            pltpu.VMEM((64, L), bf16),
            pltpu.VMEM((2 * BINS, QPAD), bf16),
            pltpu.VMEM((BINS, SPAD), f32),
            pltpu.VMEM((256, QPAD), bf16),
            pltpu.VMEM((2 * BINS, 256), f32),
            pltpu.VMEM((BINS + 8, 128), f32),
            pltpu.VMEM((NSEG, ROWS, 128), bf16),
            pltpu.VMEM((NSEG, ROWS, 128), bf16),
            pltpu.VMEM((NSEG * ROWS, 128), f32),
            pltpu.VMEM((2, NY, PER, NSEG, 128), bf16),
            pltpu.VMEM((PER, 128, 64), bf16),
            pltpu.SemaphoreType.DMA((2,)),
            pltpu.SemaphoreType.DMA,
            pltpu.SemaphoreType.DMA,
            pltpu.SemaphoreType.DMA((4, 2, 3)),
            pltpu.SemaphoreType.DMA((4, 2, 3)),
            pltpu.SemaphoreType.DMA((NY, 2)),
            pltpu.SemaphoreType.DMA((NY, 2)),
        ],
        compiler_params=pltpu.CompilerParams(
            collective_id=0, has_side_effects=True, vmem_limit_bytes=40 * 1024 * 1024
        ),
        cost_estimate=pl.CostEstimate(
            flops=600_000_000, bytes_accessed=6_000_000, transcendentals=50_000
        ),
    )(waveforms, table)


def solution(mesh):
    return jax.shard_map(
        shards,
        mesh=mesh,
        in_specs=(P("band", "blk", None),),
        out_specs=P(None, "band", "blk", None),
        check_vma=False,
    )
```

time: 252 us -> 47.9 us (0.19)
  waiting for transfers between devices: 141 us -> 0 us
  Pallas kernels: 0 us -> 43.8 us
  local copies, waits for them, and re-layouts: 41.4 us -> 3.93 us
  other arithmetic: 27.7 us -> 0 us
  blocking collectives: 21.6 us -> 0 us
  between operations: 13.5 us -> 0.01 us
  matrix products: 4.33 us -> 0 us
    all_gather x1 -> x0, waiting for transfers between devices: 141 us -> none  [shards(): lax.all_gather(local, 'blk', axis=3, tiled=True)]
    pallas_call x0 -> x1, Pallas kernels: none -> 43.8 us  [shards(): pl.pallas_call(kernel, out_shape=jax.ShapeDtypeStruct((2, PER, 64, 1024),...]
    another operation x2 -> x0, other arithmetic: 22.4 us -> none
    unnamed x6 -> x5, local copies, waits for them, and re-layouts: 26.2 us -> 3.93 us
    all_to_all x1 -> x0, blocking collectives: 21.6 us -> none  [shards(): lax.all_to_all(spectra, 'band', split_axis=1, concat_axis=2, tiled=True)]
    slice x1 -> x0, local copies, waits for them, and re-layouts: 13.9 us -> none  [pair_tile(): piece_both = jnp.concatenate([piece[0], piece[1]], axis=2)]
    dot_general x3 -> x0, matrix products: 4.33 us -> none  [the longest x1 1.9 us: pair_tile(): jnp.einsum('fsa,fsb->fab', own_both, piece_both, preferred_element_type=j...]
    convert_element_type x2 -> x0, other arithmetic: 2.65 us -> none  [the longest x1 2.63 us: shards(): return tile.astype(jnp.bfloat16)]
  transfers between devices with their start and end apart: 1 -> 0, of which waited for: 1 -> 0; matrix products, arithmetic and copies ran while one was open for 0% -> 0% of each run, Pallas kernels for 0% -> 0%
where the time goes in v1:
time: 47.9 us; the launch traced here: 47.7 us
  Pallas kernels  43.8 us (91%)
  local copies, waits for them, and re-layouts  3.93 us (8%)
    pallas_call x1, Pallas kernels, shards(): pl.pallas_call(kernel, out_shape=jax.ShapeDtypeStruct((2, PER, 64, 1024),...  43.8 us
    unnamed x5, local copies, waits for them, and re-layouts  3.93 us

profile of v1, /device:TPU:6, one launch (start us, length us, event | category | flops | bytes accessed | tf_op | source)
XLA Modules:
  0.0 47.7 jit_solution(9464353448052050475)
XLA Ops:
  0.0 0.0 copy-start
  0.0 1.3 %copy-done = bf16[768,768]{1,0:T(8,128)(2,1)S(1)} copy-done((bf16[768,768]{1,0:T(8,128)(2,1)S(1)}, bf16[768,768]{1,0:T(8,128)(2,1)}, u32[]{:S(2)}) %copy-start) | copy-done | bytes 1179672
  1.3 0.0 copy-start.1
  1.3 1.0 %copy-done.1 = bf16[1,64,3000]{2,1,0:T(8,128)(2,1)S(1)} copy-done((bf16[1,64,3000]{2,1,0:T(8,128)(2,1)S(1)}, bf16[1,64,3000]{2,1,0:T(8,128)(2,1)}, u32[]{:S(2)}) %copy-start.1) | copy-done | bytes 384024
  2.3 43.8 %shard_map.28 = bf16[2,12,64,1024]{3,2,1,0:T(8,128)(2,1)S(1)} custom-call(bf16[1,64,3000]{2,1,0:T(8,128)(2,1)S(1)} %copy-done.1, bf16[768,768]{1,0:T(8,128)(2,1)S(1)} %copy-done), custom_call_target="tpu_custom_call" | custom-call | flops 600000000 | bytes 6000000 | tf_op jit(solution)/shard_map/pallas_call | solution.py:273
  46.1 1.7 %copy.4 = bf16[2,12,64,1024]{3,2,1,0:T(8,128)(2,1)} copy(bf16[2,12,64,1024]{3,2,1,0:T(8,128)(2,1)S(1)} %shard_map.28) | data formatting | bytes 6291456
Async XLA Ops:
  0.0 1.3 %copy-start = (bf16[768,768]{1,0:T(8,128)(2,1)S(1)}, bf16[768,768]{1,0:T(8,128)(2,1)}, u32[]{:S(2)}) copy-start(bf16[768,768]{1,0:T(8,128)(2,1)} %constant.2.clone.t_hbm) | copy-start | bytes 3538948
  1.3 1.0 %copy-start.1 = (bf16[1,64,3000]{2,1,0:T(8,128)(2,1)S(1)}, bf16[1,64,3000]{2,1,0:T(8,128)(2,1)}, u32[]{:S(2)}) copy-start(bf16[1,64,3000]{2,1,0:T(8,128)(2,1)} %x_hbm.1) | copy-start | bytes 1152004

commit v2 on v1

v2 whole, which is shorter than its diff:
```python
import functools
import math

import jax
import jax.numpy as jnp
import numpy as np
import ml_dtypes
from jax import lax
from jax.experimental import pallas as pl
from jax.experimental.pallas import tpu as pltpu
from jax.sharding import PartitionSpec as P

L = 3000
BINS = 384
HALF = 64
QUARTER = 750
QPAD = 768
SPAD = 3072
PER = 12
ROWS = 16
NSEG = 32
NY = 8
MESH = pl.DeviceIdType.MESH
NHI = 16
UNROLL = 6
TABLES = 16


def make_table():
    freqs = np.arange(1, BINS + 1, dtype=np.int64)
    samples = np.arange(QUARTER, dtype=np.int64)
    phase = ((freqs[:, None] * samples[None, :]) % L).astype(np.float64) * (2.0 * math.pi / L)
    table = np.zeros((TABLES, 2 * BINS, QPAD), ml_dtypes.bfloat16)
    table[0, :BINS, :QUARTER] = np.cos(phase).astype(np.float32).astype(ml_dtypes.bfloat16)
    table[0, BINS:, :QUARTER] = (-np.sin(phase)).astype(np.float32).astype(ml_dtypes.bfloat16)
    return table


KINDS = ((0, 0), (0, 1), (1, 1))


def ring_goes(step, direction, kind):
    if step <= 3:
        return True
    return step == 4 and (kind == 2 or kind == direction)


def whiten(xv, tv, n32, x4, zs, spec, send, table_ready):
    for block in range(4):
        rows = pl.ds(16 * block, 16)
        values = xv[rows, :].astype(jnp.float32)
        centred = values - jnp.sum(values, axis=1, keepdims=True) * (1.0 / L)
        var = jnp.sum(centred * centred, axis=1, keepdims=True) * (1.0 / L)
        n32[rows, SPAD - 128 :] = jnp.zeros((16, 128), jnp.float32)
        n32[rows, :L] = centred * lax.rsqrt(var + 1e-05)
        x4[rows, :] = n32[rows, :QPAD].astype(jnp.bfloat16)
        for q in range(1, 4):
            start = QUARTER * q // 128 * 128
            off = QUARTER * q - start
            window = n32[rows, start : start + 896]
            window = pltpu.roll(window, 896 - off, 1)
            x4[pl.ds(64 * q + 16 * block, 16), :] = window[:, :QPAD].astype(jnp.bfloat16)

    table_ready()
    zs[...] = lax.dot_general(
        tv[...], x4[...], (((1,), (1,)), ((), ())), preferred_element_type=jnp.float32
    )

    shape = (96, 128)
    row = lax.broadcasted_iota(jnp.int32, shape, 0)
    lane = lax.broadcasted_iota(jnp.int32, shape, 1)
    low = lane < 64
    phase = row % 4
    even = phase % 2 == 1
    sigma = jnp.where(even, 1.0, -1.0)
    kappa = jnp.where(
        phase == 1, -1.0, jnp.where(phase == 3, 1.0, jnp.where((phase == 0) == low, 1.0, -1.0))
    )
    for part in range(4):
        rows = slice(96 * part, 96 * part + 96)
        irows = slice(BINS + 96 * part, BINS + 96 * part + 96)
        a_sum = zs[rows, :128] + sigma * zs[rows, 128:]
        b_sum = zs[irows, :128] + sigma * zs[irows, 128:]
        a_roll = pltpu.roll(a_sum, 64, 1)
        b_roll = pltpu.roll(b_sum, 64, 1)
        first = jnp.where(low, a_sum, b_roll)
        other = jnp.where(
            even, jnp.where(low, a_roll, b_sum), jnp.where(low, b_roll, a_sum)
        )
        raw = first + kappa * other
        spec[rows, :] = raw
        square = raw * raw
        power = square + pltpu.roll(square, 64, 1)
        high = power.astype(jnp.bfloat16).astype(jnp.float32)
        n32[rows, :128] = jnp.where(low, high, power - high)

    frow = lax.broadcasted_iota(jnp.int32, (BINS, BINS), 0)
    gcol = lax.broadcasted_iota(jnp.int32, (BINS, BINS), 1)
    near = jnp.where(jnp.abs(frow - gcol) <= HALF, 1.0, 0.0).astype(jnp.bfloat16)
    total = jnp.dot(
        near, n32[:BINS, :128].astype(jnp.bfloat16), preferred_element_type=jnp.float32
    )
    frow = lax.broadcasted_iota(jnp.int32, (BINS, 128), 0)
    count = jnp.minimum(frow + HALF, BINS - 1) - jnp.maximum(frow - HALF, 0) + 1
    smooth = (total + pltpu.roll(total, 64, 1)) / count.astype(jnp.float32)
    spec[:BINS, :] = spec[:BINS, :] * lax.rsqrt(smooth + 1e-05)
    spec[BINS:, :] = jnp.zeros((8, 128), jnp.float32)
    for dev in range(NSEG):
        send[dev] = spec[pl.ds(PER * dev, ROWS), :].astype(jnp.bfloat16)


def kernel(
    xv, t_hbm, o_ref,
    tv, n32, x4, zs, spec, send, recv, r32, gath, wt,
    in_sem, a_send, a_recv, s_send, s_recv, y_send, y_recv, z_send, z_recv,
):
    blk = lax.axis_index("blk")
    band = lax.axis_index("band")
    yy = blk // 2
    zz = lax.rem(blk, 2)
    hi = band // 2
    core = lax.rem(band, 2)
    right = lax.rem(yy + 1, NY) * 2 + zz
    left = lax.rem(yy + NY - 1, NY) * 2 + zz
    partner = yy * 2 + 1 - zz
    sibling = hi * 2 + 1 - core

    barrier = pltpu.get_barrier_semaphore()

    def greet(k, carry):
        pl.semaphore_signal(
            barrier,
            inc=1,
            device_id={"blk": blk, "band": lax.rem(band + k, NSEG)},
            device_id_type=MESH,
        )
        return carry

    t_copy = pltpu.make_async_copy(t_hbm.at[0], tv, in_sem)
    t_copy.start()
    for other in (left, right, partner):
        pl.semaphore_signal(
            barrier, inc=1, device_id={"blk": other, "band": band}, device_id_type=MESH
        )
    lax.fori_loop(1, NSEG, greet, 0)

    whiten(xv.at[0], tv, n32, x4, zs, spec, send, t_copy.wait)

    pl.semaphore_wait(barrier, 3 + NSEG - 1)

    def scatter(m, carry):
        for c in (0, 1):
            to = lax.rem(hi + m, NHI) * 2 + c
            pltpu.make_async_remote_copy(
                src_ref=send.at[to],
                dst_ref=recv.at[core, m],
                send_sem=a_send,
                recv_sem=a_recv.at[core],
                device_id={"blk": blk, "band": to},
                device_id_type=MESH,
            ).start()
        return carry

    lax.fori_loop(1, NHI, scatter, 0)
    to_sibling = pltpu.make_async_remote_copy(
        src_ref=send.at[sibling],
        dst_ref=recv.at[core, 0],
        send_sem=s_send,
        recv_sem=s_recv,
        device_id={"blk": blk, "band": sibling},
        device_id_type=MESH,
    )
    to_sibling.start()
    recv[core, 0] = send[band]
    others = pl.ds(1, NHI - 1)

    def collect(c):
        pltpu.make_async_copy(recv.at[c, others], recv.at[c, others], a_recv.at[c]).wait()
        pl.when(core != c)(to_sibling.wait_recv)
        for m in range(NHI):
            r32[c, pl.ds(ROWS * m, ROWS), :] = recv[c, m].astype(jnp.float32)
        for f in range(PER):
            gath[0, 0, c, f] = r32[c, pl.ds(f, NHI, stride=ROWS), :].astype(jnp.bfloat16)

    started = []

    def z_copy(slot, c):
        return pltpu.make_async_remote_copy(
            src_ref=gath.at[0, slot, c],
            dst_ref=gath.at[1, slot, c],
            send_sem=z_send.at[slot, c],
            recv_sem=z_recv.at[slot, c],
            device_id={"blk": partner, "band": band},
            device_id_type=MESH,
        )

    def y_copy(step, direction, kind):
        plane, c = KINDS[kind]
        source = (step - 1) if direction == 0 else (NY - step + 1) % NY
        target = step if direction == 0 else NY - step
        part = pl.ds(PER // 2 * direction, PER // 2) if (step, kind) == (4, 2) else pl.ds(0, PER)
        return pltpu.make_async_remote_copy(
            src_ref=gath.at[plane, source, c, part],
            dst_ref=gath.at[plane, target, c, part],
            send_sem=y_send.at[step - 1, direction, kind],
            recv_sem=y_recv.at[step - 1, direction, kind],
            device_id={"blk": (right, left)[direction], "band": band},
            device_id_type=MESH,
        )

    def start(copy):
        copy.start()
        started.append(copy)

    def stack(slots):
        columns = [
            pl.ds(pl.multiple_of(lax.rem(yy + NY - slot, NY) * 128, 128), 128) for slot in slots
        ]

        def pair(slot, f):
            g0 = jnp.concatenate([gath[zz, slot, 0, f], gath[zz, slot, 1, f]], axis=0)
            g1 = jnp.concatenate([gath[1 - zz, slot, 0, f], gath[1 - zz, slot, 1, f]], axis=0)
            top = jnp.concatenate([g0[:, :64], g1[:, :64]], axis=1)
            bottom = jnp.concatenate([g0[:, 64:], g1[:, 64:]], axis=1)
            return jnp.concatenate([top, bottom], axis=0)

        def some(i, carry):
            for u in range(UNROLL):
                f = i * UNROLL + u
                both = jnp.concatenate([pair(slot, f) for slot in slots], axis=1)
                out = jnp.dot(wt[f], both, preferred_element_type=jnp.float32)
                out = out.astype(jnp.bfloat16)
                for k, where in enumerate(columns):
                    lanes = slice(128 * k, 128 * k + 128)
                    o_ref[0, f, :, where] = out[:64, lanes]
                    o_ref[1, f, :, where] = out[64:, lanes]
            return carry

        lax.fori_loop(0, PER // UNROLL, some, 0)

    collect(0)
    for direction in (0, 1):
        start(y_copy(1, direction, 0))
    start(z_copy(0, 0))
    collect(1)
    start(z_copy(0, 1))
    for direction in (0, 1):
        start(y_copy(1, direction, 1))

    wlow = lax.broadcasted_iota(jnp.int32, (NSEG, 128), 1) < 64
    for f in range(PER):
        own = jnp.concatenate(
            [r32[c, pl.ds(f, NHI, stride=ROWS), :] for c in (0, 1)], axis=0
        ) * (1.0 / NSEG)
        turned = pltpu.roll(own, 64, 1)
        turned = jnp.where(wlow, turned, -turned)
        wt[f] = jnp.transpose(jnp.concatenate([own, turned], axis=0)).astype(jnp.bfloat16)

    z_copy(0, 1).wait_recv()
    for direction in (0, 1):
        start(y_copy(1, direction, 2))

    previous = (0,)
    for step in range(1, 5):
        for kind in range(3):
            for direction in (0, 1):
                if not ring_goes(step, direction, kind):
                    continue
                slot = step if direction == 0 else NY - step
                y_copy(step, direction, kind).wait_recv()
                if ring_goes(step + 1, direction, kind):
                    start(y_copy(step + 1, direction, kind))
                if kind == 0:
                    start(z_copy(slot, 0))
        for slot in previous:
            z_copy(slot, 0).wait_recv()
        stack(previous)
        previous = (step, NY - step) if step < 4 else (4,)
    z_copy(4, 0).wait_recv()
    stack(previous)

    for copy in started:
        copy.wait_send()
    to_sibling.wait_send()
    for half in (0, 1):
        rest = pl.ds(0, NHI - 1)
        pltpu.make_async_copy(send.at[rest], send.at[rest], a_send).wait()


def shards(waveforms):
    table = jnp.asarray(make_table())
    bf16, f32 = jnp.bfloat16, jnp.float32
    return pl.pallas_call(
        kernel,
        out_shape=jax.ShapeDtypeStruct((2, PER, 64, 1024), bf16),
        in_specs=[
            pl.BlockSpec(memory_space=pltpu.VMEM),
            pl.BlockSpec(memory_space=pl.ANY),
        ],
        out_specs=pl.BlockSpec(memory_space=pltpu.VMEM),
        scratch_shapes=[
            pltpu.VMEM((2 * BINS, QPAD), bf16),
            pltpu.VMEM((BINS, SPAD), f32),
            pltpu.VMEM((256, QPAD), bf16),
            pltpu.VMEM((2 * BINS, 256), f32),
            pltpu.VMEM((BINS + 8, 128), f32),
            pltpu.VMEM((NSEG, ROWS, 128), bf16),
            pltpu.VMEM((2, NHI, ROWS, 128), bf16),
            pltpu.VMEM((2, NHI * ROWS, 128), f32),
            pltpu.VMEM((2, NY, 2, PER, NHI, 128), bf16),
            pltpu.VMEM((PER, 128, 64), bf16),
            pltpu.SemaphoreType.DMA,
            pltpu.SemaphoreType.DMA,
            pltpu.SemaphoreType.DMA((2,)),
            pltpu.SemaphoreType.DMA,
            pltpu.SemaphoreType.DMA,
            pltpu.SemaphoreType.DMA((4, 2, 3)),
            pltpu.SemaphoreType.DMA((4, 2, 3)),
            pltpu.SemaphoreType.DMA((NY, 2)),
            pltpu.SemaphoreType.DMA((NY, 2)),
        ],
        compiler_params=pltpu.CompilerParams(
            collective_id=0, has_side_effects=True, vmem_limit_bytes=44 * 1024 * 1024
        ),
        cost_estimate=pl.CostEstimate(
            flops=600_000_000, bytes_accessed=6_000_000, transcendentals=50_000
        ),
    )(waveforms, table)


def solution(mesh):
    return jax.shard_map(
        shards,
        mesh=mesh,
        in_specs=(P("band", "blk", None),),
        out_specs=P(None, "band", "blk", None),
        check_vma=False,
    )
```

time: 47.9 us -> 43.5 us (0.908)
  Pallas kernels: 43.8 us -> 40.4 us
  local copies, waits for them, and re-layouts: 3.93 us -> 2.66 us
    pallas_call x1, Pallas kernels: 43.8 us -> 40.4 us  [shards(): pl.pallas_call(kernel, out_shape=jax.ShapeDtypeStruct((2, PER, 64, 1024),...]
    unnamed x5 -> x3, local copies, waits for them, and re-layouts: 3.93 us -> 2.66 us
where the time goes in v2:
time: 43.5 us; the launch traced here: 43.1 us
  Pallas kernels  40.4 us (93%)
  local copies, waits for them, and re-layouts  2.66 us (6%)
    pallas_call x1, Pallas kernels, shards(): pl.pallas_call(kernel, out_shape=jax.ShapeDtypeStruct((2, PER, 64, 1024),...  40.4 us
    unnamed x3, local copies, waits for them, and re-layouts  2.66 us

profile of v2, /device:TPU:6, one launch (start us, length us, event | category | flops | bytes accessed | tf_op | source)
XLA Modules:
  0.0 43.1 jit_solution(10462635346572304415)
XLA Ops:
  0.0 0.0 copy-start
  0.0 1.0 %copy-done = bf16[1,64,3000]{2,1,0:T(8,128)(2,1)S(1)} copy-done((bf16[1,64,3000]{2,1,0:T(8,128)(2,1)S(1)}, bf16[1,64,3000]{2,1,0:T(8,128)(2,1)}, u32[]{:S(2)}) %copy-start) | copy-done | bytes 384024
  1.0 40.4 %shard_map.28 = bf16[2,12,64,1024]{3,2,1,0:T(8,128)(2,1)S(1)} custom-call(bf16[1,64,3000]{2,1,0:T(8,128)(2,1)S(1)} %copy-done, bf16[16,768,768]{2,1,0:T(8,128)(2,1)} %constant.2.clone.t_hbm), custom_call_target="tpu_custom_call" | custom-call | flops 600000000 | bytes 6000000 | tf_op jit(solution)/shard_map/pallas_call | solution.py:293
  41.4 1.7 %copy.4 = bf16[2,12,64,1024]{3,2,1,0:T(8,128)(2,1)} copy(bf16[2,12,64,1024]{3,2,1,0:T(8,128)(2,1)S(1)} %shard_map.28) | data formatting | bytes 6291456
Async XLA Ops:
  0.0 1.0 %copy-start = (bf16[1,64,3000]{2,1,0:T(8,128)(2,1)S(1)}, bf16[1,64,3000]{2,1,0:T(8,128)(2,1)}, u32[]{:S(2)}) copy-start(bf16[1,64,3000]{2,1,0:T(8,128)(2,1)} %xv.1) | copy-start | bytes 1152004

commit v3 on v2

--- a/solution.py
+++ b/solution.py
@@ -1,4 +1,4 @@
-import functools
+import heapq
 import math
 
 import jax
@@ -22,7 +22,6 @@
 NY = 8
 MESH = pl.DeviceIdType.MESH
 NHI = 16
-UNROLL = 6
 TABLES = 16
 
 
@@ -36,13 +35,90 @@
     return table
 
 
-KINDS = ((0, 0), (0, 1), (1, 1))
-
-
-def ring_goes(step, direction, kind):
-    if step <= 3:
-        return True
-    return step == 4 and (kind == 2 or kind == direction)
+PARTS = 3
+PIECES = [(c, p) for c in (0, 1) for p in range(PARTS)]
+Y_FIRST = PIECES[:4]
+DIAGONAL = True
+SKIP = True
+DY = (1, -1, 2, -2)
+LATENCY, HOP, LATE, GAP = 2.6, 0.55, 1.0, 0.1
+
+
+def make_plan():
+    unit, cost = 1.07 / PARTS, 0.06
+    last = {}
+    for plane in (0, 1):
+        for piece in PIECES:
+            if plane == 0 or piece not in Y_FIRST:
+                last[plane, *piece] = (1, -1)[len(last) % 2]
+    free = {1: 0.0, -1: 0.0, 0: 0.0}
+    arrivals, plan = [], []
+    now = 0.0
+
+    def start(plane, slot, piece, dy, dz):
+        nonlocal now
+        now += cost
+        sign = (dy > 0) - (dy < 0)
+        links = ([sign] if dy else []) + ([0] if dz else [])
+        begin = max([free[k] for k in links] + [now])
+        for k in links:
+            free[k] = max(free[k], begin) + unit * (abs(dy) if k else 1)
+        copy = (plane, slot, *piece, dy, dz)
+        arrival = begin + unit + LATENCY + HOP * (abs(dy) + dz - 1)
+        heapq.heappush(arrivals, (arrival, len(plan), copy))
+        plan.append(("start", copy))
+
+    for core in (0, 1):
+        mine = [piece for piece in PIECES if piece[0] == core]
+        if core == 1:
+            plan.append(("second",))
+            now = max(now, LATE)
+        for piece in mine:
+            if piece not in Y_FIRST:
+                start(0, 0, piece, 0, 1)
+        for piece in mine:
+            for sign in (1, -1):
+                start(0, 0, piece, sign, 0)
+            if piece not in Y_FIRST and DIAGONAL:
+                for sign in (1, -1):
+                    start(0, 0, piece, sign, 1)
+        for piece in mine:
+            if piece in Y_FIRST:
+                start(0, 0, piece, 0, 1)
+    missing = {(slot, p): 4 if slot else 2 for slot in range(NY) for p in range(PARTS)}
+    groups = [(0,), (1, 7), (2, 6), (3, 5), (4,)]
+    ready = []
+    while arrivals:
+        while ready and arrivals[0][0] - now > GAP:
+            plan.append(ready.pop(0))
+            now += GAP
+        when, _, copy = heapq.heappop(arrivals)
+        now = max(now, when) + cost
+        plan.append(("wait", copy))
+        plane, slot, core, part, dy, dz = copy
+        piece = (core, part)
+        plane, slot = (plane + dz) % 2, (slot + dy) % NY
+        sign = (dy > 0) - (dy < 0)
+        first_cross = plane == 1 and piece not in Y_FIRST
+        if dy == 0:
+            if slot == 0 and first_cross and not DIAGONAL:
+                for sign in (1, -1):
+                    start(1, 0, piece, sign, 0)
+        elif plane == 0 or first_cross:
+            distance = min(slot, NY - slot)
+            if distance < 3:
+                start(plane, slot, piece, sign, 0)
+            if last[plane, core, part] == sign and distance == (2 if SKIP else 3):
+                start(plane, slot, piece, (2 if SKIP else 1) * sign, 0)
+            if plane == 0 and piece in Y_FIRST:
+                start(0, slot, piece, 0, 1)
+        missing[slot, part] -= 1
+        for group in groups:
+            if slot in group and not any(missing[k, part] for k in group):
+                ready.append(("stack", group, part))
+    plan.extend(ready)
+    assert not any(missing.values())
+    return plan
 
 
 def whiten(xv, tv, n32, x4, zs, spec, send, table_ready):
@@ -112,7 +188,7 @@
 def kernel(
     xv, t_hbm, o_ref,
     tv, n32, x4, zs, spec, send, recv, r32, gath, wt,
-    in_sem, a_send, a_recv, s_send, s_recv, y_send, y_recv, z_send, z_recv,
+    in_sem, a_send, a_recv, s_send, s_recv, g_send, g_recv,
 ):
     blk = lax.axis_index("blk")
     band = lax.axis_index("band")
@@ -120,9 +196,8 @@
     zz = lax.rem(blk, 2)
     hi = band // 2
     core = lax.rem(band, 2)
-    right = lax.rem(yy + 1, NY) * 2 + zz
-    left = lax.rem(yy + NY - 1, NY) * 2 + zz
     partner = yy * 2 + 1 - zz
+    near = [lax.rem(yy + dy + NY, NY) * 2 + z for dy in DY for z in (zz, 1 - zz)] + [partner]
     sibling = hi * 2 + 1 - core
 
     barrier = pltpu.get_barrier_semaphore()
@@ -138,7 +213,7 @@
 
     t_copy = pltpu.make_async_copy(t_hbm.at[0], tv, in_sem)
     t_copy.start()
-    for other in (left, right, partner):
+    for other in near:
         pl.semaphore_signal(
             barrier, inc=1, device_id={"blk": other, "band": band}, device_id_type=MESH
         )
@@ -146,7 +221,7 @@
 
     whiten(xv.at[0], tv, n32, x4, zs, spec, send, t_copy.wait)
 
-    pl.semaphore_wait(barrier, 3 + NSEG - 1)
+    pl.semaphore_wait(barrier, len(near) + NSEG - 1)
 
     def scatter(m, carry):
         for c in (0, 1):
@@ -182,37 +257,24 @@
         for f in range(PER):
             gath[0, 0, c, f] = r32[c, pl.ds(f, NHI, stride=ROWS), :].astype(jnp.bfloat16)
 
-    started = []
-
-    def z_copy(slot, c):
+    plan = make_plan()
+    copies = [entry[1] for entry in plan if entry[0] == "start"]
+
+    def described(copy):
+        plane, slot, c, part, dy, dz = copy
+        k = copies.index(copy)
+        rows = pl.ds(PER // PARTS * part, PER // PARTS)
+        to = lax.rem(yy + dy + NY, NY) * 2 + (1 - zz if dz else zz)
         return pltpu.make_async_remote_copy(
-            src_ref=gath.at[0, slot, c],
-            dst_ref=gath.at[1, slot, c],
-            send_sem=z_send.at[slot, c],
-            recv_sem=z_recv.at[slot, c],
-            device_id={"blk": partner, "band": band},
+            src_ref=gath.at[plane, slot, c, rows],
+            dst_ref=gath.at[(plane + dz) % 2, (slot + dy) % NY, c, rows],
+            send_sem=g_send.at[k],
+            recv_sem=g_recv.at[k],
+            device_id={"blk": to, "band": band},
             device_id_type=MESH,
         )
 
-    def y_copy(step, direction, kind):
-        plane, c = KINDS[kind]
-        source = (step - 1) if direction == 0 else (NY - step + 1) % NY
-        target = step if direction == 0 else NY - step
-        part = pl.ds(PER // 2 * direction, PER // 2) if (step, kind) == (4, 2) else pl.ds(0, PER)
-        return pltpu.make_async_remote_copy(
-            src_ref=gath.at[plane, source, c, part],
-            dst_ref=gath.at[plane, target, c, part],
-            send_sem=y_send.at[step - 1, direction, kind],
-            recv_sem=y_recv.at[step - 1, direction, kind],
-            device_id={"blk": (right, left)[direction], "band": band},
-            device_id_type=MESH,
-        )
-
-    def start(copy):
-        copy.start()
-        started.append(copy)
-
-    def stack(slots):
+    def stack(slots, part):
         columns = [
             pl.ds(pl.multiple_of(lax.rem(yy + NY - slot, NY) * 128, 128), 128) for slot in slots
         ]
@@ -224,63 +286,42 @@
             bottom = jnp.concatenate([g0[:, 64:], g1[:, 64:]], axis=1)
             return jnp.concatenate([top, bottom], axis=0)
 
-        def some(i, carry):
-            for u in range(UNROLL):
-                f = i * UNROLL + u
-                both = jnp.concatenate([pair(slot, f) for slot in slots], axis=1)
-                out = jnp.dot(wt[f], both, preferred_element_type=jnp.float32)
-                out = out.astype(jnp.bfloat16)
-                for k, where in enumerate(columns):
-                    lanes = slice(128 * k, 128 * k + 128)
-                    o_ref[0, f, :, where] = out[:64, lanes]
-                    o_ref[1, f, :, where] = out[64:, lanes]
-            return carry
-
-        lax.fori_loop(0, PER // UNROLL, some, 0)
+        for f in range(PER // PARTS * part, PER // PARTS * (part + 1)):
+            both = jnp.concatenate([pair(slot, f) for slot in slots], axis=1)
+            out = jnp.dot(wt[f], both, preferred_element_type=jnp.float32)
+            out = out.astype(jnp.bfloat16)
+            for k, where in enumerate(columns):
+                lanes = slice(128 * k, 128 * k + 128)
+                o_ref[0, f, :, where] = out[:64, lanes]
+                o_ref[1, f, :, where] = out[64:, lanes]
+
+    def turn_own():
+        wlow = lax.broadcasted_iota(jnp.int32, (NSEG, 128), 1) < 64
+        for f in range(PER):
+            own = jnp.concatenate(
+                [r32[c, pl.ds(f, NHI, stride=ROWS), :] for c in (0, 1)], axis=0
+            ) * (1.0 / NSEG)
+            turned = pltpu.roll(own, 64, 1)
+            turned = jnp.where(wlow, turned, -turned)
+            wt[f] = jnp.transpose(jnp.concatenate([own, turned], axis=0)).astype(jnp.bfloat16)
 
     collect(0)
-    for direction in (0, 1):
-        start(y_copy(1, direction, 0))
-    start(z_copy(0, 0))
-    collect(1)
-    start(z_copy(0, 1))
-    for direction in (0, 1):
-        start(y_copy(1, direction, 1))
-
-    wlow = lax.broadcasted_iota(jnp.int32, (NSEG, 128), 1) < 64
-    for f in range(PER):
-        own = jnp.concatenate(
-            [r32[c, pl.ds(f, NHI, stride=ROWS), :] for c in (0, 1)], axis=0
-        ) * (1.0 / NSEG)
-        turned = pltpu.roll(own, 64, 1)
-        turned = jnp.where(wlow, turned, -turned)
-        wt[f] = jnp.transpose(jnp.concatenate([own, turned], axis=0)).astype(jnp.bfloat16)
-
-    z_copy(0, 1).wait_recv()
-    for direction in (0, 1):
-        start(y_copy(1, direction, 2))
-
-    previous = (0,)
-    for step in range(1, 5):
-        for kind in range(3):
-            for direction in (0, 1):
-                if not ring_goes(step, direction, kind):
-                    continue
-                slot = step if direction == 0 else NY - step
-                y_copy(step, direction, kind).wait_recv()
-                if ring_goes(step + 1, direction, kind):
-                    start(y_copy(step + 1, direction, kind))
-                if kind == 0:
-                    start(z_copy(slot, 0))
-        for slot in previous:
-            z_copy(slot, 0).wait_recv()
-        stack(previous)
-        previous = (step, NY - step) if step < 4 else (4,)
-    z_copy(4, 0).wait_recv()
-    stack(previous)
-
-    for copy in started:
-        copy.wait_send()
+    turned_yet = False
+    for entry in plan:
+        if entry[0] == "second":
+            collect(1)
+        elif entry[0] == "start":
+            described(entry[1]).start()
+        elif entry[0] == "wait":
+            if not turned_yet:
+                turn_own()
+                turned_yet = True
+            described(entry[1]).wait_recv()
+        else:
+            stack(*entry[1:])
+
+    for copy in copies:
+        described(copy).wait_send()
     to_sibling.wait_send()
     for half in (0, 1):
         rest = pl.ds(0, NHI - 1)
@@ -290,6 +331,7 @@
 def shards(waveforms):
     table = jnp.asarray(make_table())
     bf16, f32 = jnp.bfloat16, jnp.float32
+    n_copies = sum(entry[0] == "start" for entry in make_plan())
     return pl.pallas_call(
         kernel,
         out_shape=jax.ShapeDtypeStruct((2, PER, 64, 1024), bf16),
@@ -314,10 +356,8 @@
             pltpu.SemaphoreType.DMA((2,)),
             pltpu.SemaphoreType.DMA,
             pltpu.SemaphoreType.DMA,
-            pltpu.SemaphoreType.DMA((4, 2, 3)),
-            pltpu.SemaphoreType.DMA((4, 2, 3)),
-            pltpu.SemaphoreType.DMA((NY, 2)),
-            pltpu.SemaphoreType.DMA((NY, 2)),
+            pltpu.SemaphoreType.DMA((n_copies,)),
+            pltpu.SemaphoreType.DMA((n_copies,)),
         ],
         compiler_params=pltpu.CompilerParams(
             collective_id=0, has_side_effects=True, vmem_limit_bytes=44 * 1024 * 1024

time: 43.5 us -> 41.1 us (0.945)
  Pallas kernels: 40.4 us -> 38.1 us
    pallas_call x1, Pallas kernels: 40.4 us -> 38.1 us  [shards(): pl.pallas_call(kernel, out_shape=jax.ShapeDtypeStruct((2, PER, 64, 1024),...]
where the time goes in v3:
time: 41.1 us; the launch traced here: 40.8 us
  Pallas kernels  38.1 us (93%)
  local copies, waits for them, and re-layouts  2.66 us (6%)
    pallas_call x1, Pallas kernels, shards(): pl.pallas_call(kernel, out_shape=jax.ShapeDtypeStruct((2, PER, 64, 1024),...  38.1 us
    unnamed x3, local copies, waits for them, and re-layouts  2.66 us

profile of v3, /device:TPU:6, one launch (start us, length us, event | category | flops | bytes accessed | tf_op | source)
XLA Modules:
  0.0 40.8 jit_solution(6478965930494077187)
XLA Ops:
  0.0 0.0 copy-start
  0.0 1.0 %copy-done = bf16[1,64,3000]{2,1,0:T(8,128)(2,1)S(1)} copy-done((bf16[1,64,3000]{2,1,0:T(8,128)(2,1)S(1)}, bf16[1,64,3000]{2,1,0:T(8,128)(2,1)}, u32[]{:S(2)}) %copy-start) | copy-done | bytes 384024
  1.0 38.1 %shard_map.28 = bf16[2,12,64,1024]{3,2,1,0:T(8,128)(2,1)S(1)} custom-call(bf16[1,64,3000]{2,1,0:T(8,128)(2,1)S(1)} %copy-done, bf16[16,768,768]{2,1,0:T(8,128)(2,1)} %constant.2.clone.t_hbm), custom_call_target="tpu_custom_call" | custom-call | flops 600000000 | bytes 6000000 | tf_op jit(solution)/shard_map/pallas_call | solution.py:335
  39.1 1.7 %copy.4 = bf16[2,12,64,1024]{3,2,1,0:T(8,128)(2,1)} copy(bf16[2,12,64,1024]{3,2,1,0:T(8,128)(2,1)S(1)} %shard_map.28) | data formatting | bytes 6291456
Async XLA Ops:
  0.0 1.0 %copy-start = (bf16[1,64,3000]{2,1,0:T(8,128)(2,1)S(1)}, bf16[1,64,3000]{2,1,0:T(8,128)(2,1)}, u32[]{:S(2)}) copy-start(bf16[1,64,3000]{2,1,0:T(8,128)(2,1)} %xv.1) | copy-start | bytes 1152004

commit v4 on v3

--- a/solution.py
+++ b/solution.py
@@ -36,12 +36,15 @@
 
 
 PARTS = 3
-PIECES = [(c, p) for c in (0, 1) for p in range(PARTS)]
+PIECES = [(group, p) for group in (0, 1) for p in range(PARTS)]
 Y_FIRST = PIECES[:4]
 DIAGONAL = True
 SKIP = True
 DY = (1, -1, 2, -2)
-LATENCY, HOP, LATE, GAP = 2.6, 0.55, 1.0, 0.1
+LATENCY, HOP, LATE = 3.2, 0.55, 3.0
+ORDER = (1, 0, 2, 3)
+TURN = 0.8
+GAP, WORK, BACKLOG = 0.1, 0.22, 0
 
 
 def make_plan():
@@ -60,19 +63,16 @@
         now += cost
         sign = (dy > 0) - (dy < 0)
         links = ([sign] if dy else []) + ([0] if dz else [])
-        begin = max([free[k] for k in links] + [now])
+        first = max([free[k] for k in links] + [now])
         for k in links:
-            free[k] = max(free[k], begin) + unit * (abs(dy) if k else 1)
+            free[k] = max(free[k], first) + unit * (abs(dy) if k else 1)
         copy = (plane, slot, *piece, dy, dz)
-        arrival = begin + unit + LATENCY + HOP * (abs(dy) + dz - 1)
+        arrival = first + unit + LATENCY + HOP * (abs(dy) + dz - 1)
         heapq.heappush(arrivals, (arrival, len(plan), copy))
         plan.append(("start", copy))
 
-    for core in (0, 1):
-        mine = [piece for piece in PIECES if piece[0] == core]
-        if core == 1:
-            plan.append(("second",))
-            now = max(now, LATE)
+    def begin(group):
+        mine = [piece for piece in PIECES if piece[0] == group]
         for piece in mine:
             if piece not in Y_FIRST:
                 start(0, 0, piece, 0, 1)
@@ -85,15 +85,24 @@
         for piece in mine:
             if piece in Y_FIRST:
                 start(0, 0, piece, 0, 1)
+
+    begin(0)
+    heapq.heappush(arrivals, (LATE, -1, None))
     missing = {(slot, p): 4 if slot else 2 for slot in range(NY) for p in range(PARTS)}
     groups = [(0,), (1, 7), (2, 6), (3, 5), (4,)]
     ready = []
     while arrivals:
         while ready and arrivals[0][0] - now > GAP:
             plan.append(ready.pop(0))
-            now += GAP
+            now += WORK
         when, _, copy = heapq.heappop(arrivals)
         now = max(now, when) + cost
+        if copy is None:
+            plan.append(("second",))
+            begin(1)
+            plan.append(("turn",))
+            now += TURN
+            continue
         plan.append(("wait", copy))
         plane, slot, core, part, dy, dz = copy
         piece = (core, part)
@@ -116,6 +125,9 @@
         for group in groups:
             if slot in group and not any(missing[k, part] for k in group):
                 ready.append(("stack", group, part))
+        if len(ready) > BACKLOG:
+            plan.append(ready.pop(0))
+            now += WORK
     plan.extend(ready)
     assert not any(missing.values())
     return plan
@@ -194,68 +206,72 @@
     band = lax.axis_index("band")
     yy = blk // 2
     zz = lax.rem(blk, 2)
-    hi = band // 2
+    xx = band // 8
+    zhi = lax.rem(band // 2, 4)
     core = lax.rem(band, 2)
     partner = yy * 2 + 1 - zz
     near = [lax.rem(yy + dy + NY, NY) * 2 + z for dy in DY for z in (zz, 1 - zz)] + [partner]
-    sibling = hi * 2 + 1 - core
+    sibling = band + 1 - 2 * core
 
     barrier = pltpu.get_barrier_semaphore()
-
-    def greet(k, carry):
-        pl.semaphore_signal(
-            barrier,
-            inc=1,
-            device_id={"blk": blk, "band": lax.rem(band + k, NSEG)},
-            device_id_type=MESH,
-        )
-        return carry
 
     t_copy = pltpu.make_async_copy(t_hbm.at[0], tv, in_sem)
     t_copy.start()
+    for dz in (0, 1, 3, 2):
+        for dx in (2, 1, 3, 0):
+            for c in (0, 1) if dx or dz else ():
+                to = lax.rem(xx + dx, 4) * 8 + lax.rem(zhi + dz, 4) * 2 + c
+                pl.semaphore_signal(
+                    barrier, inc=1, device_id={"blk": blk, "band": to}, device_id_type=MESH
+                )
     for other in near:
         pl.semaphore_signal(
             barrier, inc=1, device_id={"blk": other, "band": band}, device_id_type=MESH
         )
-    lax.fori_loop(1, NSEG, greet, 0)
+    pl.semaphore_signal(
+        barrier, inc=1, device_id={"blk": blk, "band": sibling}, device_id_type=MESH
+    )
 
     whiten(xv.at[0], tv, n32, x4, zs, spec, send, t_copy.wait)
 
     pl.semaphore_wait(barrier, len(near) + NSEG - 1)
 
-    def scatter(m, carry):
+    def send_to(dx, dz):
+        chip = lax.rem(xx + dx, 4) * 8 + lax.rem(zhi + dz, 4) * 2
         for c in (0, 1):
-            to = lax.rem(hi + m, NHI) * 2 + c
             pltpu.make_async_remote_copy(
-                src_ref=send.at[to],
-                dst_ref=recv.at[core, m],
+                src_ref=send.at[chip + c],
+                dst_ref=recv.at[dz // 2, 4 * dx + 2 * (dz % 2) + core],
                 send_sem=a_send,
-                recv_sem=a_recv.at[core],
-                device_id={"blk": blk, "band": to},
+                recv_sem=a_recv.at[dz // 2],
+                device_id={"blk": blk, "band": chip + c},
                 device_id_type=MESH,
             ).start()
-        return carry
-
-    lax.fori_loop(1, NHI, scatter, 0)
+
+    for dz in ORDER:
+        for dx in (2, 1, 3, 0):
+            if dx or dz:
+                send_to(dx, dz)
     to_sibling = pltpu.make_async_remote_copy(
         src_ref=send.at[sibling],
-        dst_ref=recv.at[core, 0],
+        dst_ref=recv.at[0, core],
         send_sem=s_send,
         recv_sem=s_recv,
         device_id={"blk": blk, "band": sibling},
         device_id_type=MESH,
     )
     to_sibling.start()
-    recv[core, 0] = send[band]
-    others = pl.ds(1, NHI - 1)
-
-    def collect(c):
-        pltpu.make_async_copy(recv.at[c, others], recv.at[c, others], a_recv.at[c]).wait()
-        pl.when(core != c)(to_sibling.wait_recv)
-        for m in range(NHI):
-            r32[c, pl.ds(ROWS * m, ROWS), :] = recv[c, m].astype(jnp.float32)
+    recv[0, core] = send[band]
+
+    def collect(group):
+        came = pl.ds(0, NHI) if group else pl.ds(2, NHI - 2)
+        pltpu.make_async_copy(recv.at[group, came], recv.at[group, came], a_recv.at[group]).wait()
+        if group == 0:
+            to_sibling.wait_recv()
+        for k in range(NHI):
+            r32[group, pl.ds(ROWS * k, ROWS), :] = recv[group, k].astype(jnp.float32)
         for f in range(PER):
-            gath[0, 0, c, f] = r32[c, pl.ds(f, NHI, stride=ROWS), :].astype(jnp.bfloat16)
+            gath[0, 0, group, f] = r32[group, pl.ds(f, NHI, stride=ROWS), :].astype(jnp.bfloat16)
 
     plan = make_plan()
     copies = [entry[1] for entry in plan if entry[0] == "start"]
@@ -268,7 +284,7 @@
         return pltpu.make_async_remote_copy(
             src_ref=gath.at[plane, slot, c, rows],
             dst_ref=gath.at[(plane + dz) % 2, (slot + dy) % NY, c, rows],
-            send_sem=g_send.at[k],
+            send_sem=g_send,
             recv_sem=g_recv.at[k],
             device_id={"blk": to, "band": band},
             device_id_type=MESH,
@@ -306,22 +322,26 @@
             wt[f] = jnp.transpose(jnp.concatenate([own, turned], axis=0)).astype(jnp.bfloat16)
 
     collect(0)
-    turned_yet = False
     for entry in plan:
         if entry[0] == "second":
             collect(1)
+        elif entry[0] == "turn":
+            turn_own()
         elif entry[0] == "start":
             described(entry[1]).start()
         elif entry[0] == "wait":
-            if not turned_yet:
-                turn_own()
-                turned_yet = True
             described(entry[1]).wait_recv()
         else:
             stack(*entry[1:])
 
-    for copy in copies:
-        described(copy).wait_send()
+    whole = 4 * NY * PARTS
+    for _ in range(len(copies) // whole):
+        pltpu.make_async_copy(gath, gath, g_send).wait()
+    size = PER // PARTS
+    spare = len(copies) % whole
+    for piece in range(spare):
+        one = gath.at[0, 0, 0, pl.ds(0, size)]
+        pltpu.make_async_copy(one, one, g_send).wait()
     to_sibling.wait_send()
     for half in (0, 1):
         rest = pl.ds(0, NHI - 1)
@@ -356,7 +376,7 @@
             pltpu.SemaphoreType.DMA((2,)),
             pltpu.SemaphoreType.DMA,
             pltpu.SemaphoreType.DMA,
-            pltpu.SemaphoreType.DMA((n_copies,)),
+            pltpu.SemaphoreType.DMA,
             pltpu.SemaphoreType.DMA((n_copies,)),
         ],
         compiler_params=pltpu.CompilerParams(

time: 41.1 us -> 39.3 us (0.956)
  Pallas kernels: 38.1 us -> 36.3 us
    pallas_call x1, Pallas kernels: 38.1 us -> 36.3 us  [shards(): pl.pallas_call(kernel, out_shape=jax.ShapeDtypeStruct((2, PER, 64, 1024),...]
where the time goes in v4:
time: 39.3 us; the launch traced here: 39 us
  Pallas kernels  36.3 us (92%)
  local copies, waits for them, and re-layouts  2.66 us (7%)
    pallas_call x1, Pallas kernels, shards(): pl.pallas_call(kernel, out_shape=jax.ShapeDtypeStruct((2, PER, 64, 1024),...  36.3 us
    unnamed x3, local copies, waits for them, and re-layouts  2.66 us

profile of v4, /device:TPU:6, one launch (start us, length us, event | category | flops | bytes accessed | tf_op | source)
XLA Modules:
  0.0 39.0 jit_solution(17604528201630769513)
XLA Ops:
  0.0 0.0 copy-start
  0.0 1.0 %copy-done = bf16[1,64,3000]{2,1,0:T(8,128)(2,1)S(1)} copy-done((bf16[1,64,3000]{2,1,0:T(8,128)(2,1)S(1)}, bf16[1,64,3000]{2,1,0:T(8,128)(2,1)}, u32[]{:S(2)}) %copy-start) | copy-done | bytes 384024
  1.0 36.3 %shard_map.28 = bf16[2,12,64,1024]{3,2,1,0:T(8,128)(2,1)S(1)} custom-call(bf16[1,64,3000]{2,1,0:T(8,128)(2,1)S(1)} %copy-done, bf16[16,768,768]{2,1,0:T(8,128)(2,1)} %constant.2.clone.t_hbm), custom_call_target="tpu_custom_call" | custom-call | flops 600000000 | bytes 6000000 | tf_op jit(solution)/shard_map/pallas_call | solution.py:355
  37.3 1.7 %copy.4 = bf16[2,12,64,1024]{3,2,1,0:T(8,128)(2,1)} copy(bf16[2,12,64,1024]{3,2,1,0:T(8,128)(2,1)S(1)} %shard_map.28) | data formatting | bytes 6291456
Async XLA Ops:
  0.0 1.0 %copy-start = (bf16[1,64,3000]{2,1,0:T(8,128)(2,1)S(1)}, bf16[1,64,3000]{2,1,0:T(8,128)(2,1)}, u32[]{:S(2)}) copy-start(bf16[1,64,3000]{2,1,0:T(8,128)(2,1)} %xv.1) | copy-start | bytes 1152004
